TPU v7x, 1024 devices: a whole 4x8x16 slice. The times are simulated.
1024 devices in a mesh: hst: 8 (over y_lo, core), outer: 128 (over z, x, y_hi).
Axes of the slice: x: 4, y: 8 (y_hi: 2, y_lo: 4; y = y_hi * 4 + y_lo), z: 16, core: 2. Of those that a mesh axis runs over, the one named last changes fastest.
Arguments:
- tokens: bfloat16 [131072, 4096], P(('hst', 'outer')), may hold values from -24 to 24
- weight_codes: int32 [4096, 512], P('hst'), may hold values from -127 to 127
- weight_scales: float32 [32, 512], P('hst'), may hold values from 0.0001 to 0.0006
- grad_codes: int32 [131072, 512], P(('hst', 'outer')), may hold values from -8 to 7
- grad_scales: float32 [131072, 4], P(('hst', 'outer')), may hold values from 0.05 to 0.5
Outputs:
- values: bfloat16 [131072, 512], P(('hst', 'outer'))
- tokens_grad: bfloat16 [131072, 4096], P(('hst', 'outer'))
- weight_grad: float32 [4096, 512], P(('hst', 'outer'))
All inputs are finite; a program needn't handle non-finite values.
Results may differ from a plain program's by a relative error of at most 0.015.
Values may be sent and summed in bfloat16 or wider, within the bound.
A program may use at most 64 MiB of HBM per device.

v0:
```python
import jax
import jax.numpy as jnp
from jax import lax
from jax.sharding import PartitionSpec as P


def rounded_term(source, upstream):
    term = lax.dot_general(
        source, upstream, (((0,), (0,)), ((), ())), preferred_element_type=jnp.float32
    )
    rounded = lax.optimization_barrier(term.astype(jnp.bfloat16))
    return rounded.astype(jnp.float32)


def body(tokens, weight_codes, weight_scales, grad_codes, grad_scales):
    tok_rows, model_width = tokens.shape
    local_rows, kv_width = weight_codes.shape
    scale_rows = weight_scales.shape[0]
    head_count = grad_scales.shape[1]
    coded = weight_codes.astype(jnp.float32).reshape(scale_rows, local_rows // scale_rows, kv_width)
    weight_piece = (
        (coded * weight_scales[:, None, :]).reshape(local_rows, kv_width).astype(jnp.bfloat16)
    )
    grad_coded = grad_codes.astype(jnp.float32).reshape(
        tok_rows, head_count, kv_width // head_count
    )
    upstream = (
        (grad_coded * grad_scales[:, :, None]).reshape(tok_rows, kv_width).astype(jnp.bfloat16)
    )
    full_weight = lax.all_gather(weight_piece, "hst", axis=0, tiled=True)
    values = jnp.dot(tokens, full_weight, preferred_element_type=jnp.float32).astype(jnp.bfloat16)
    tokens_grad = lax.dot_general(
        upstream, full_weight, (((1,), (1,)), ((), ())), preferred_element_type=jnp.float32
    ).astype(jnp.bfloat16)
    host_part = lax.psum_scatter(
        rounded_term(tokens, upstream).astype(jnp.bfloat16), "hst", scatter_dimension=0, tiled=True
    ).astype(jnp.float32)
    weight_grad = lax.psum_scatter(host_part, "outer", scatter_dimension=0, tiled=True)
    return (values, tokens_grad, weight_grad)


def solution(mesh):
    return jax.shard_map(
        body,
        mesh=mesh,
        in_specs=(
            P(("hst", "outer"), None),
            P("hst", None),
            P("hst", None),
            P(("hst", "outer"), None),
            P(("hst", "outer"), None),
        ),
        out_specs=(P(("hst", "outer"), None), P(("hst", "outer"), None), P(("hst", "outer"), None)),
        check_vma=False,
    )
```

profile of v0, /device:TPU:8, one launch (start us, length us, event | category | flops | bytes accessed | tf_op | source)
XLA Modules:
  0.0 1025.7 jit_solution(148994215209208020)
XLA Ops:
  7.2 0.0 copy-start
  7.2 0.0 all-gather.2.cloned.1.call-start
  7.2 2.2 fusion.2
  9.5 0.0 all-gather.2.cloned.1.call-update
  9.5 0.0 reduce-scatter.3.cloned.1.call-start
  9.5 0.8 copy.11
  10.3 0.2 mul.25
  10.5 1.0 fusion.3
  11.5 0.0 copy-done
  11.5 3.2 fusion
  14.8 0.0 reduce-scatter.3.cloned.1.call-update
  14.8 1.3 dynamic-slice
  16.7 60.6 %all-gather.2.cloned.1.call-done = bf16[4096,512]{1,0:T(8,128)(2,1)} async-done(((bf16[512,512]{1,0:T(8,128)(2,1)}), bf16[4096,512]{1,0:T(8,128)(2,1)}) %all-gather.2.cloned.1.call-update) | async-done | bytes 4194320 | tf_op jit(solution)/shard_map/all_gather | solution.py:30
  77.3 3.5 fusion.1
  80.8 0.8 copy.12
  81.6 4.6 convolution_convert_fusion.1
  86.2 56.4 %reduce-scatter.3.cloned.1.call-done = bf16[512,512]{0,1:T(8,128)(2,1)} async-done(((bf16[4096,512]{0,1:T(8,128)(2,1)}), bf16[512,512]{0,1:T(8,128)(2,1)}) %reduce-scatter.3.cloned.1.call-update) | async-done | bytes 524304 | tf_op jit(solution)/shard_map/reduce_scatter | solution.py:35
  142.6 875.4 %all-reduce.2 = f32[512,512]{0,1:T(8,128)S(1)} all-reduce(bf16[512,512]{0,1:T(8,128)(2,1)} %reduce-scatter.3.cloned.1.call-done), channel_id=3, replica_groups=mesh['hst'=8,'outer'=128] {'outer'}, use_global_device_ids=true, to_apply=%region_1.0.clone | all-reduce | flops 262144 | bytes 1572864
  1018.0 0.1 constant_dynamic-slice_fusion
  1018.2 0.7 copy.13
Async XLA Ops:
  7.2 4.3 copy-start
  7.2 70.1 %all-gather.2.cloned.1.call-start = ((), (), s32[]{:S(2)}) async-start(), calls=%async_computation.1 | async-start | bytes 4718592 | tf_op jit(solution)/shard_map/all_gather | solution.py:30
  9.5 133.1 %reduce-scatter.3.cloned.1.call-start = ((), (), s32[]{:S(2)}) async-start(), calls=%async_computation.2 | async-start | bytes 4718592 | tf_op jit(solution)/shard_map/reduce_scatter | solution.py:35
Sparse Core Ops, SparseCore 0:
  11.2 66.0 all-gather.1
  80.7 61.8 reduce-scatter.2
where the time goes:
time: 1030 us
  blocking collectives  875 us (85%)
  waiting for transfers between devices  117 us (11%)
  between operations  14.7 us (1%)
  matrix products  11.4 us (1%)
    unnamed x1, blocking collectives  875 us
    all_gather x1, waiting for transfers between devices, body(): full_weight = lax.all_gather(weight_piece, 'hst', axis=0, tiled=True)  60.6 us
    reduce_scatter x1, waiting for transfers between devices, body(): lax.psum_scatter(rounded_term(tokens, upstream).astype(jnp.bfloat16), 'hs...  56.4 us
  transfers between devices with their start and end apart: 2, of which 2 were waited for; matrix products, arithmetic and copies ran while one was open for 1% of the time, Pallas kernels for 0%

commit v1 on v0

v1 whole, which is shorter than its diff:
```python
import jax
import jax.numpy as jnp
from jax import lax
from jax.experimental import pallas as pl
from jax.experimental.pallas import tpu as pltpu
from jax.sharding import PartitionSpec as P

F32, BF16 = jnp.float32, jnp.bfloat16
NX, NY, NZ = 4, 8, 16
LO = 4
TOK, D, KV, ROWS, HEADS = 128, 4096, 512, 512, 4
HALF = ROWS // 2
FIRST = (256, 512, 768, 896)
COUNT = (128, 128, 64, 64)


def kernel(
    tok_hbm, wc_hbm, ws_ref, gc_hbm, gs_ref,
    val_ref, tg_ref, wg_ref,
    tok, wc, gc, wbuf, trecv, urecv, vacc, term, xsend, xown, xrecv, ysend, yrecv, zsend, zrecv,
    in_sem, tsend, trcv, ownsem, usend, urcv, ucsend, ucrcv,
    wsend, wrcv, wcsend, wcrcv, xs_sem, xr_sem, ys_sem, yr_sem, zs_sem, zr_sem,
):
    h, o = lax.axis_index("hst"), lax.axis_index("outer")
    c, ylo = lax.rem(h, 2), h // 2
    yhi, x, z = lax.rem(o, 2), lax.rem(o // 2, NX), o // (2 * NX)
    y = yhi * LO + ylo
    oc = 1 - c

    def dev(x, y, z, c):
        return (lax.rem(y, LO) * 2 + c, (z * NX + x) * 2 + y // LO)

    def at_z(step):
        return lax.rem(z + step + NZ, NZ)

    def at_y(step):
        return lax.rem(y + step + NY, NY)

    def at_x(step):
        return lax.rem(x + step, NX)

    def pair_of(y):
        return (y // LO) * LO + lax.rem(2 * lax.rem(y, LO) + 1, 5)

    def unpair(p):
        return (p // LO) * LO + lax.rem(3 * lax.rem(p, LO) + 2, 5)

    def remote(src, dst, ssem, rsem, to):
        return pltpu.make_async_remote_copy(
            src_ref=src, dst_ref=dst, send_sem=ssem, recv_sem=rsem,
            device_id=to, device_id_type=pl.DeviceIdType.MESH,
        )

    pair = pair_of(y)
    finals = [
        dev(x, g * LO + lax.rem(z, LO), 2 * pair + b, c) for b in range(2) for g in range(2)
    ]
    sources = [dev(x, unpair(z // 2), ylo + LO * g, c) for g in range(4)]
    zsteps = (1, -1, 2, -2)

    load_tok = pltpu.make_async_copy(tok_hbm, tok, in_sem.at[0])
    load_wc = pltpu.make_async_copy(wc_hbm, wc, in_sem.at[1])
    load_gc = pltpu.make_async_copy(gc_hbm, gc, in_sem.at[2])
    load_gc.start()
    load_wc.start()
    load_tok.start()

    barrier = pltpu.get_barrier_semaphore()
    partners = [dev(x, y, z, oc)]
    partners += [dev(x, at_y(s), z, c) for s in range(1, NY)]
    partners += [dev(x, y, at_z(s), cc) for s in zsteps for cc in (c, oc)]
    partners += [dev(at_x(s), y, z, c) for s in range(1, NX)]
    partners += finals + sources
    for p in partners:
        pl.semaphore_signal(barrier, inc=1, device_id=p, device_id_type=pl.DeviceIdType.MESH)
    pl.semaphore_wait(barrier, len(partners))

    def columns(zz, cc):
        return pl.ds(pl.multiple_of((lax.rem(zz, LO) * 2 + cc) * ROWS, ROWS), ROWS)

    own_tok = pltpu.make_async_copy(
        tok_hbm.at[:, columns(z, c)], trecv.at[pl.ds(0, TOK)], ownsem
    )
    own_tok.start()
    other_tok = remote(
        tok_hbm.at[:, columns(z, oc)], trecv.at[pl.ds(TOK, TOK)], tsend.at[8], trcv.at[8],
        dev(x, y, z, oc),
    )
    other_tok.start()
    tok_copies = []
    for i, s in enumerate(zsteps):
        first = 64 if s == -2 else 0
        for j, cc in enumerate((c, oc)):
            copy = remote(
                tok_hbm.at[pl.ds(first, COUNT[i]), columns(at_z(s), cc)],
                trecv.at[pl.ds(FIRST[i] + j * COUNT[i], COUNT[i])],
                tsend.at[2 * i + j], trcv.at[2 * i + j], dev(x, y, at_z(s), cc),
            )
            tok_copies.append(copy)

    load_gc.wait()
    for k in range(HEADS):
        lanes = slice(k * 128, (k + 1) * 128)
        urecv[0:TOK, lanes] = (gc[:, lanes].astype(F32) * gs_ref[:, k : k + 1]).astype(BF16)
    other_up = remote(
        urecv.at[pl.ds(0, TOK)], urecv.at[pl.ds(TOK, TOK)], ucsend.at[4], ucrcv.at[4],
        dev(x, y, z, oc),
    )
    other_up.start()
    up_copies = []
    for i, s in enumerate(zsteps):
        first = 64 if s == -2 else 0
        copy = remote(
            urecv.at[pl.ds(first, COUNT[i])], urecv.at[pl.ds(FIRST[i], COUNT[i])],
            usend.at[i], urcv.at[i], dev(x, y, at_z(s), c),
        )
        copy.start()
        up_copies.append(copy)
    for copy in tok_copies:
        copy.start()

    load_wc.wait()
    for b in range(ROWS // 128):
        rows = slice(b * 128, (b + 1) * 128)
        wbuf[h, rows, :] = (wc[rows, :].astype(F32) * ws_ref[b : b + 1, :]).astype(BF16)

    def part(ylo_of, cc, half):
        return wbuf.at[ylo_of * 2 + cc, pl.ds(half * HALF, HALF)]

    left, right, far = lax.rem(ylo + 3, LO), lax.rem(ylo + 1, LO), lax.rem(ylo + 2, LO)
    to_left, to_right, to_core = dev(x, at_y(-1), z, c), dev(x, at_y(1), z, c), dev(x, y, z, oc)
    w_copies = []

    def send_w(which, half, ssem, rsem, to):
        src = part(which, c, half)
        copy = remote(src, src, ssem, rsem, to)
        copy.start()
        w_copies.append(copy)
        return copy

    send_w(ylo, 0, wsend.at[0], wrcv.at[0], to_right)
    send_w(ylo, 1, wsend.at[3], wrcv.at[3], to_left)
    send_w(ylo, 1, wsend.at[1], wrcv.at[1], to_right)
    send_w(ylo, 0, wsend.at[2], wrcv.at[2], to_left)
    send_w(ylo, 0, wcsend.at[6], wcrcv.at[6], to_core)
    send_w(ylo, 1, wcsend.at[7], wcrcv.at[7], to_core)
    where = ((left, 0), (left, 1), (right, 0), (right, 1), (far, 0), (far, 1), (ylo, 0), (ylo, 1))

    def arrived(i):
        which, half = where[i]
        ref = part(which, c, half)
        remote(ref, ref, wsend.at[i], wrcv.at[i], to_core).wait_recv()

    def arrived_core(i):
        which, half = where[i]
        ref = part(which, oc, half)
        remote(ref, ref, wcsend.at[i], wcrcv.at[i], to_core).wait_recv()

    def pass_on(i):
        which, half = where[i]
        send_w(which, half, wcsend.at[i], wcrcv.at[i], to_core)

    load_tok.wait()
    vacc[...] = jnp.zeros_like(vacc)

    def multiply(i, cc):
        which, half = where[i]
        slot = which * 2 + cc
        lanes = pl.ds(pl.multiple_of(slot * ROWS + half * HALF, HALF), HALF)
        piece = wbuf[slot, half * HALF : (half + 1) * HALF, :]
        vacc[...] += jnp.dot(tok[:, lanes], piece, preferred_element_type=F32)
        tg_ref[:, lanes] = lax.dot_general(
            urecv[0:TOK, :], piece, (((1,), (1,)), ((), ())), preferred_element_type=F32
        ).astype(BF16)

    def add_term(first, fresh):
        @pl.loop(0, 2)
        def _(m):
            lanes = pl.ds(pl.multiple_of(m * 256, 256), 256)
            product = lax.dot_general(
                trecv[first : first + 256, lanes], urecv[first : first + 256, :],
                (((0,), (0,)), ((), ())), preferred_element_type=F32,
            )
            if fresh:
                term[lanes, :] = product
            else:
                term[lanes, :] += product

    multiply(6, c)
    multiply(7, c)
    arrived(0)
    send_w(left, 0, wsend.at[4], wrcv.at[4], to_right)
    pass_on(0)
    arrived(3)
    send_w(right, 1, wsend.at[5], wrcv.at[5], to_left)
    pass_on(3)

    for i in range(4):
        up_copies[i].wait_recv()
        rows = urecv.at[pl.ds(FIRST[i], COUNT[i])]
        copy = remote(
            rows, urecv.at[pl.ds(FIRST[i] + COUNT[i], COUNT[i])], ucsend.at[i], ucrcv.at[i], to_core
        )
        copy.start()
        up_copies.append(copy)

    own_tok.wait()
    other_tok.wait_recv()
    other_up.wait_recv()
    add_term(0, True)
    arrived_core(6)
    multiply(6, oc)
    arrived_core(7)
    multiply(7, oc)
    multiply(0, c)
    multiply(3, c)
    arrived(1)
    pass_on(1)
    arrived(2)
    pass_on(2)
    multiply(1, c)
    multiply(2, c)
    arrived_core(0)
    multiply(0, oc)
    arrived_core(3)
    multiply(3, oc)

    def neighbours(i):
        tok_copies[2 * i].wait_recv()
        tok_copies[2 * i + 1].wait_recv()
        up_copies[4 + i].wait_recv()

    neighbours(0)
    add_term(FIRST[0], False)
    neighbours(1)
    add_term(FIRST[1], False)
    arrived(4)
    pass_on(4)
    arrived(5)
    pass_on(5)
    neighbours(2)
    neighbours(3)
    add_term(FIRST[2], False)

    def of_x(xx):
        rows = [
            term[pl.ds(pl.multiple_of(a * 32 + xx * 8, 8), 8), :] for a in range(NZ)
        ]
        return jnp.concatenate(rows, axis=0)

    x_copies = []
    for s in (2, 1, 3):
        xsend[s - 1] = of_x(at_x(s)).astype(BF16)
        copy = remote(
            xsend.at[s - 1], xrecv.at[s - 1], xs_sem.at[s - 1], xr_sem.at[s - 1],
            dev(at_x(s), y, z, c),
        )
        copy.start()
        x_copies.append(copy)
    xown[...] = of_x(x)

    arrived_core(1)
    multiply(1, oc)
    arrived_core(2)
    multiply(2, oc)
    multiply(4, c)
    multiply(5, c)

    for copy in x_copies:
        copy.wait_recv()
    total = xown[...]
    for s in range(NX - 1):
        total += xrecv[s].astype(F32)
    for p in range(NY):
        ysend[p] = total[p * 16 : (p + 1) * 16, :].astype(BF16)
    y_copies = []
    for s in (4, 3, 5, 2, 6, 1, 7):
        copy = remote(
            ysend.at[pair_of(at_y(s))], yrecv.at[s - 1], ys_sem.at[s - 1], yr_sem.at[s - 1],
            dev(x, at_y(s), z, c),
        )
        copy.start()
        y_copies.append(copy)

    arrived_core(4)
    multiply(4, oc)
    arrived_core(5)
    multiply(5, oc)
    val_ref[...] = vacc[...].astype(BF16)

    for copy in y_copies:
        copy.wait_recv()
    total = ysend[pair].astype(F32)
    for s in range(NY - 1):
        total += yrecv[s].astype(F32)
    zsend[0] = total[0:8, :]
    zsend[1] = total[8:16, :]
    z_copies = []
    for i, to in enumerate(finals):
        copy = remote(
            zsend.at[i // 2], zrecv.at[z // LO], zs_sem.at[i], zr_sem.at[z // LO], to
        )
        copy.start()
        z_copies.append(copy)
    for g in range(4):
        remote(zsend.at[0], zrecv.at[g], zs_sem.at[g], zr_sem.at[g], to_core).wait_recv()
    final = (zrecv[0] + zrecv[1]) + (zrecv[2] + zrecv[3])
    wg_ref[...] = jnp.where(yhi == 0, final[0:4, :], final[4:8, :])

    other_tok.wait_send()
    other_up.wait_send()
    for copy in tok_copies + up_copies + w_copies + x_copies + y_copies + z_copies:
        copy.wait_send()


def body(tokens, weight_codes, weight_scales, grad_codes, grad_scales):
    any_space = pl.BlockSpec(memory_space=pl.ANY)
    vmem = pl.BlockSpec(memory_space=pltpu.VMEM)
    dma = pltpu.SemaphoreType.DMA
    return pl.pallas_call(
        kernel,
        out_shape=(
            jax.ShapeDtypeStruct((TOK, KV), BF16),
            jax.ShapeDtypeStruct((TOK, D), BF16),
            jax.ShapeDtypeStruct((4, KV), F32),
        ),
        in_specs=[any_space, any_space, vmem, any_space, vmem],
        out_specs=(vmem, vmem, vmem),
        scratch_shapes=[
            pltpu.VMEM((TOK, D), BF16),
            pltpu.VMEM((ROWS, KV), jnp.int32),
            pltpu.VMEM((TOK, KV), jnp.int32),
            pltpu.VMEM((8, ROWS, KV), BF16),
            pltpu.VMEM((1024, ROWS), BF16),
            pltpu.VMEM((1024, KV), BF16),
            pltpu.VMEM((TOK, KV), F32),
            pltpu.VMEM((ROWS, KV), F32),
            pltpu.VMEM((NX - 1, 128, KV), BF16),
            pltpu.VMEM((128, KV), F32),
            pltpu.VMEM((NX - 1, 128, KV), BF16),
            pltpu.VMEM((NY, 16, KV), BF16),
            pltpu.VMEM((NY - 1, 16, KV), BF16),
            pltpu.VMEM((2, 8, KV), F32),
            pltpu.VMEM((4, 8, KV), F32),
            dma((3,)),
            dma((9,)), dma((9,)), dma,
            dma((4,)), dma((4,)), dma((5,)), dma((5,)),
            dma((6,)), dma((6,)), dma((8,)), dma((8,)),
            dma((3,)), dma((3,)), dma((7,)), dma((7,)), dma((4,)), dma((4,)),
        ],
        compiler_params=pltpu.CompilerParams(
            collective_id=0, has_side_effects=True, vmem_limit_bytes=40 * 1024 * 1024
        ),
    )(tokens, weight_codes, weight_scales, grad_codes, grad_scales)


def solution(mesh):
    return jax.shard_map(
        body,
        mesh=mesh,
        in_specs=(
            P(("hst", "outer"), None),
            P("hst", None),
            P("hst", None),
            P(("hst", "outer"), None),
            P(("hst", "outer"), None),
        ),
        out_specs=(P(("hst", "outer"), None), P(("hst", "outer"), None), P(("hst", "outer"), None)),
        check_vma=False,
    )
```

time: 1030 us -> 77.4 us (0.08)
  the two profiles are of different devices: /device:TPU:8 before, /device:TPU:48 now
where the time goes in v1:
time: 77.4 us; the launch traced here: 77.1 us
  Pallas kernels  70 us (90%)
  local copies, waits for them, and re-layouts  6.42 us (8%)
    pallas_call x1, Pallas kernels, body(): pl.pallas_call(kernel, out_shape=(jax.ShapeDtypeStruct((TOK, KV), BF16),...  70 us
    unnamed x12, local copies, waits for them, and re-layouts  6.42 us

profile of v1, /device:TPU:48, one launch (start us, length us, event | category | flops | bytes accessed | tf_op | source)
XLA Modules:
  0.0 77.1 jit_solution(10575708126477524977)
XLA Ops:
  0.6 0.0 copy-start.3
  0.6 0.8 %copy.8.gs_ref = f32[128,4]{1,0:T(8,128)S(1)} copy(f32[128,4]{0,1:T(4,128)} %param.9) | data formatting | bytes 4096 | tf_op args[4]
  1.4 0.0 copy-done.3
  1.4 0.0 copy-start
  1.5 1.2 %copy-done = bf16[128,4096]{1,0:T(8,128)(2,1)S(1)} copy-done((bf16[128,4096]{1,0:T(8,128)(2,1)S(1)}, bf16[128,4096]{1,0:T(8,128)(2,1)}, u32[]{:S(2)}) %copy-start) | copy-done | bytes 1048600
  2.7 0.0 copy-start.1
  2.7 1.2 %copy-done.1 = s32[512,512]{1,0:T(8,128)S(1)} copy-done((s32[512,512]{1,0:T(8,128)S(1)}, s32[512,512]{1,0:T(8,128)}, u32[]{:S(2)}) %copy-start.1) | copy-done | bytes 1048600
  3.9 0.0 copy-start.2
  3.9 0.9 %copy-done.2 = s32[128,512]{1,0:T(8,128)S(1)} copy-done((s32[128,512]{1,0:T(8,128)S(1)}, s32[128,512]{1,0:T(8,128)}, u32[]{:S(2)}) %copy-start.2) | copy-done | bytes 262168
  4.8 70.0 %shard_map.76 = (bf16[128,512]{1,0:T(8,128)(2,1)S(1)}, bf16[128,4096]{1,0:T(8,128)(2,1)S(1)}, f32[4,512]{1,0:T(4,128)S(1)}) custom-call(bf16[128,4096]{1,0:T(8,128)(2,1)S(1)} %copy-done, s32[512,512]{1,0:T(8,128)S(1)} %copy-done.1, f32[4,512]{1,0:T(4,128)S(1)} %copy-done.3, s32[128,512]{1,0:T(8,128)S(1)} %copy-done.2, f32[128,4]{1,0:T(8,128)S(1)} %copy.8.gs_ref), custom_call_target="tpu_custom_call" | custom-call | tf_op jit(solution)/shard_map/pallas_call | solution.py:320
  74.9 0.7 copy.12
  75.5 1.0 %copy.13 = bf16[128,4096]{1,0:T(8,128)(2,1)} copy(bf16[128,4096]{1,0:T(8,128)(2,1)S(1)} %get-tuple-element.7) | data formatting | bytes 2097152
  76.5 0.6 copy.14
Async XLA Ops:
  0.6 0.8 %copy-start.3 = (f32[4,512]{1,0:T(4,128)S(1)}, f32[4,512]{1,0:T(4,128)}, u32[]{:S(2)}) copy-start(f32[4,512]{1,0:T(4,128)} %ws_ref.1) | copy-start | bytes 24580
  1.4 1.2 %copy-start = (bf16[128,4096]{1,0:T(8,128)(2,1)S(1)}, bf16[128,4096]{1,0:T(8,128)(2,1)}, u32[]{:S(2)}) copy-start(bf16[128,4096]{1,0:T(8,128)(2,1)} %tok_hbm.1) | copy-start | bytes 3145732
  2.7 1.2 %copy-start.1 = (s32[512,512]{1,0:T(8,128)S(1)}, s32[512,512]{1,0:T(8,128)}, u32[]{:S(2)}) copy-start(s32[512,512]{1,0:T(8,128)} %wc_hbm.1) | copy-start | bytes 3145732
  3.9 0.9 %copy-start.2 = (s32[128,512]{1,0:T(8,128)S(1)}, s32[128,512]{1,0:T(8,128)}, u32[]{:S(2)}) copy-start(s32[128,512]{1,0:T(8,128)} %gc_hbm.1) | copy-start | bytes 786436

commit v2 on v1

v2 whole, which is shorter than its diff:
```python
import jax
import jax.numpy as jnp
from jax import lax
from jax.experimental import pallas as pl
from jax.experimental.pallas import tpu as pltpu
from jax.sharding import PartitionSpec as P

F32, BF16 = jnp.float32, jnp.bfloat16
NX, NY, NZ = 4, 8, 16
LO = 4
TOK, D, KV, ROWS, HEADS = 128, 4096, 512, 512, 4
HALF = ROWS // 2
XSTEPS, XFIRST, XCOUNT = (1, 3, 2), (256, 512, 768), (128, 128, 128)
ZSTEPS, ZFIRST, ZCOUNT = (1, -1, 2, -2), (256, 512, 768, 896), (128, 128, 64, 64)


def kernel(
    tok_hbm, wc_hbm, ws_ref, gc_hbm, gs_ref,
    val_hbm, tg_hbm, wg_ref,
    val_ref, tg_ref, tok, wc, gc, wbuf, tx, tz, ux, uz, vacc, term_x, term_z,
    zout, zin, zown, xout, xin, xown, ysend, yrecv, fsend, frecv,
    in_sem, own_sem, core_tsend, core_trcv, tx_send, tx_rcv, tz_send, tz_rcv,
    ux_send, ux_rcv, uz_send, uz_rcv, uc_send, uc_rcv,
    wsend, wrcv, wcsend, wcrcv, z_send, z_rcv, x_send, x_rcv, y_send, y_rcv, f_send, f_rcv, out_sem,
):
    h, o = lax.axis_index("hst"), lax.axis_index("outer")
    c, ylo = lax.rem(h, 2), h // 2
    yhi, x, z = lax.rem(o, 2), lax.rem(o // 2, NX), o // (2 * NX)
    y = yhi * LO + ylo
    oc = 1 - c
    klass = lax.rem(z, LO)

    def dev(x, y, z, c):
        return (lax.rem(y, LO) * 2 + c, (z * NX + x) * 2 + y // LO)

    def at_z(step):
        return lax.rem(z + step + NZ, NZ)

    def at_y(step):
        return lax.rem(y + step + NY, NY)

    def at_x(step):
        return lax.rem(x + step, NX)

    def remote(src, dst, ssem, rsem, to):
        return pltpu.make_async_remote_copy(
            src_ref=src, dst_ref=dst, send_sem=ssem, recv_sem=rsem,
            device_id=to, device_id_type=pl.DeviceIdType.MESH,
        )

    def signal(to):
        pl.semaphore_signal(barrier, inc=1, device_id=to, device_id_type=pl.DeviceIdType.MESH)

    by_x = ylo < 2
    final_x = jnp.where(by_x, klass, x)
    final_q = jnp.where(by_x, x, klass)
    finals = [dev(final_x, y, final_q * LO + i, c) for i in range(LO)]
    final_self = [(final_x == x) & (final_q * LO + i == z) for i in range(LO)]
    source_x = jnp.where(by_x, z // LO, x)
    source_k = jnp.where(by_x, x, z // LO)
    sources = [dev(source_x, y, source_k + LO * g, c) for g in range(4)]
    source_self = [(source_x == x) & (source_k + LO * g == z) for g in range(4)]
    loner = (final_x == x) & (final_q == z // LO)

    load_tok = pltpu.make_async_copy(tok_hbm, tok, in_sem.at[0])
    load_wc = pltpu.make_async_copy(wc_hbm, wc, in_sem.at[1])
    load_gc = pltpu.make_async_copy(gc_hbm, gc, in_sem.at[2])
    load_gc.start()
    load_wc.start()
    load_tok.start()

    def columns(ylo_of, cc, q):
        return pl.ds(pl.multiple_of(((ylo_of * 2 + cc) * 4 + q) * 128, 128), 128)

    own_copies = []
    for j in range(2):
        lanes = pl.ds(j * 128, 128)
        own_copies.append(pltpu.make_async_copy(
            tok_hbm.at[:, columns(j, c, x)], tx.at[pl.ds(0, TOK), lanes], own_sem.at[j]
        ))
        own_copies.append(pltpu.make_async_copy(
            tok_hbm.at[:, columns(2 + j, c, klass)], tz.at[pl.ds(0, TOK), lanes], own_sem.at[2 + j]
        ))
    for copy in own_copies:
        copy.start()

    barrier = pltpu.get_barrier_semaphore()
    partners = [dev(x, y, z, oc)]
    partners += [dev(x, at_y(s), z, c) for s in range(1, NY)]
    partners += [dev(x, y, at_z(s), cc) for s in ZSTEPS for cc in (c, oc)]
    partners += [dev(at_x(s), y, z, cc) for s in XSTEPS for cc in (c, oc)]
    for p in partners:
        signal(p)
    for p, same in zip(finals + sources, final_self + source_self):
        @pl.when(jnp.logical_not(same))
        def _(p=p):
            signal(p)
    pl.semaphore_wait(barrier, jnp.where(loner, len(partners) + 6, len(partners) + 8))

    core_copies, tx_copies, tz_copies = [], [], []
    for j in range(2):
        lanes = pl.ds(j * 128, 128)
        core_copies.append(remote(
            tok_hbm.at[:, columns(j, oc, x)], tx.at[pl.ds(TOK, TOK), lanes],
            core_tsend.at[j], core_trcv.at[j], dev(x, y, z, oc),
        ))
        core_copies.append(remote(
            tok_hbm.at[:, columns(2 + j, oc, klass)], tz.at[pl.ds(TOK, TOK), lanes],
            core_tsend.at[2 + j], core_trcv.at[2 + j], dev(x, y, z, oc),
        ))
    for i, s in enumerate(XSTEPS):
        for k, cc in enumerate((c, oc)):
            for j in range(2):
                tx_copies.append(remote(
                    tok_hbm.at[:, columns(j, cc, at_x(s))],
                    tx.at[pl.ds(XFIRST[i] + k * XCOUNT[i], XCOUNT[i]), pl.ds(j * 128, 128)],
                    tx_send.at[4 * i + 2 * k + j], tx_rcv.at[4 * i + 2 * k + j],
                    dev(at_x(s), y, z, cc),
                ))
    for i, s in enumerate(ZSTEPS):
        first = 64 if s == -2 else 0
        for k, cc in enumerate((c, oc)):
            for j in range(2):
                tz_copies.append(remote(
                    tok_hbm.at[pl.ds(first, ZCOUNT[i]), columns(2 + j, cc, lax.rem(at_z(s), LO))],
                    tz.at[pl.ds(ZFIRST[i] + k * ZCOUNT[i], ZCOUNT[i]), pl.ds(j * 128, 128)],
                    tz_send.at[4 * i + 2 * k + j], tz_rcv.at[4 * i + 2 * k + j],
                    dev(x, y, at_z(s), cc),
                ))
    for copy in tx_copies[8:] + tz_copies[8:] + core_copies:
        copy.start()

    load_gc.wait()
    scales = gs_ref[...].T
    for k in range(HEADS):
        lanes = slice(k * 128, (k + 1) * 128)
        ux[0:TOK, lanes] = (gc[:, lanes].astype(F32) * scales[:, k : k + 1]).astype(BF16)
    to_core = dev(x, y, z, oc)
    up_own = remote(
        ux.at[pl.ds(0, TOK)], ux.at[pl.ds(TOK, TOK)], uc_send.at[7], uc_rcv.at[7], to_core
    )
    ux_copies = [
        remote(
            ux.at[pl.ds(0, TOK)], ux.at[pl.ds(XFIRST[i], TOK)],
            ux_send.at[i], ux_rcv.at[i], dev(at_x(s), y, z, c),
        )
        for i, s in enumerate(XSTEPS)
    ]
    uz_copies = [
        remote(
            ux.at[pl.ds(64 if s == -2 else 0, ZCOUNT[i])], uz.at[pl.ds(ZFIRST[i], ZCOUNT[i])],
            uz_send.at[i], uz_rcv.at[i], dev(x, y, at_z(s), c),
        )
        for i, s in enumerate(ZSTEPS)
    ]
    for copy in ux_copies + uz_copies + [up_own]:
        copy.start()
    for copy in tx_copies[:8] + tz_copies[:8]:
        copy.start()
    uc_copies = [
        remote(
            ux.at[pl.ds(XFIRST[i], TOK)], ux.at[pl.ds(XFIRST[i] + TOK, TOK)],
            uc_send.at[i], uc_rcv.at[i], to_core,
        )
        for i in range(3)
    ] + [
        remote(
            uz.at[pl.ds(ZFIRST[i], ZCOUNT[i])], uz.at[pl.ds(ZFIRST[i] + ZCOUNT[i], ZCOUNT[i])],
            uc_send.at[3 + i], uc_rcv.at[3 + i], to_core,
        )
        for i in range(4)
    ]

    load_wc.wait()
    for b in range(ROWS // 128):
        rows = slice(b * 128, (b + 1) * 128)
        wbuf[h, rows, :] = (wc[rows, :].astype(F32) * ws_ref[b : b + 1, :]).astype(BF16)

    def part(ylo_of, cc, half):
        return wbuf.at[ylo_of * 2 + cc, pl.ds(half * HALF, HALF)]

    left, right, far = lax.rem(ylo + 3, LO), lax.rem(ylo + 1, LO), lax.rem(ylo + 2, LO)
    to_left, to_right = dev(x, at_y(-1), z, c), dev(x, at_y(1), z, c)
    w_copies = []

    def send_w(which, half, ssem, rsem, to):
        src = part(which, c, half)
        copy = remote(src, src, ssem, rsem, to)
        copy.start()
        w_copies.append(copy)

    send_w(ylo, 0, wsend.at[0], wrcv.at[0], to_right)
    send_w(ylo, 1, wsend.at[3], wrcv.at[3], to_left)
    send_w(ylo, 1, wsend.at[1], wrcv.at[1], to_right)
    send_w(ylo, 0, wsend.at[2], wrcv.at[2], to_left)
    send_w(ylo, 0, wcsend.at[6], wcrcv.at[6], to_core)
    send_w(ylo, 1, wcsend.at[7], wcrcv.at[7], to_core)
    where = ((left, 0), (left, 1), (right, 0), (right, 1), (far, 0), (far, 1), (ylo, 0), (ylo, 1))

    def arrived(i):
        which, half = where[i]
        ref = part(which, c, half)
        remote(ref, ref, wsend.at[i], wrcv.at[i], to_core).wait_recv()

    def arrived_core(i):
        which, half = where[i]
        ref = part(which, oc, half)
        remote(ref, ref, wcsend.at[i], wcrcv.at[i], to_core).wait_recv()

    def pass_on(i):
        which, half = where[i]
        send_w(which, half, wcsend.at[i], wcrcv.at[i], to_core)

    load_tok.wait()
    vacc[...] = jnp.zeros_like(vacc)

    def multiply(i, cc):
        which, half = where[i]
        slot = which * 2 + cc
        lanes = pl.ds(pl.multiple_of(slot * ROWS + half * HALF, HALF), HALF)
        piece = wbuf[slot, half * HALF : (half + 1) * HALF, :]
        vacc[...] += jnp.dot(tok[:, lanes], piece, preferred_element_type=F32)
        tg_ref[:, lanes] = lax.dot_general(
            ux[0:TOK, :], piece, (((1,), (1,)), ((), ())), preferred_element_type=F32
        ).astype(BF16)

    def product(tokens, upstream, first):
        return lax.dot_general(
            tokens[first : first + 256, :], upstream[first : first + 256, :],
            (((0,), (0,)), ((), ())), preferred_element_type=F32,
        )

    multiply(6, c)
    multiply(7, c)
    arrived(0)
    send_w(left, 0, wsend.at[4], wrcv.at[4], to_right)
    pass_on(0)
    arrived(3)
    send_w(right, 1, wsend.at[5], wrcv.at[5], to_left)
    pass_on(3)

    def up_pass_on(copy, i):
        copy.wait_recv()
        uc_copies[i].start()

    for i in (0, 1):
        up_pass_on(ux_copies[i], i)
        up_pass_on(uz_copies[i], 3 + i)

    for copy in own_copies:
        copy.wait()
    for copy in core_copies + [up_own]:
        copy.wait_recv()
    term_x[...] = product(tx, ux, 0)
    term_z[...] = product(tz, ux, 0)
    up_pass_on(ux_copies[2], 2)
    up_pass_on(uz_copies[2], 5)
    up_pass_on(uz_copies[3], 6)
    arrived_core(6)
    multiply(6, oc)
    arrived_core(7)
    multiply(7, oc)
    multiply(0, c)
    multiply(3, c)

    def wait_x(i):
        for copy in tx_copies[4 * i : 4 * i + 4] + [uc_copies[i]]:
            copy.wait_recv()

    def wait_z(i):
        for copy in tz_copies[4 * i : 4 * i + 4] + [uc_copies[3 + i]]:
            copy.wait_recv()

    for i in range(2):
        wait_x(i)
        term_x[...] += product(tx, ux, XFIRST[i])
        wait_z(i)
        term_z[...] += product(tz, uz, ZFIRST[i])

    def of_x(term, xx):
        rows = [term[pl.ds(pl.multiple_of(a * 32 + xx * 8, 8), 8), :] for a in range(8)]
        return jnp.concatenate(rows, axis=0)

    wait_x(2)
    term_x[...] += product(tx, ux, XFIRST[2])
    zout_copies = []
    for i, s in enumerate((2, 1, -1)):
        zout[i] = of_x(term_x, lax.rem(at_z(s), LO)).astype(BF16)
        if s == 2:
            pieces = ((0, 32, 2, 2, 2), (32, 32, -2, 2, 3))
        else:
            pieces = ((0, 64, s, 0 if s == 1 else 1, 0 if s == 1 else 1),)
        for first, count, step, slot, sem in pieces:
            copy = remote(
                zout.at[i, pl.ds(first, count)], zin.at[slot, pl.ds(first, count)],
                z_send.at[sem], z_rcv.at[sem], dev(x, y, at_z(step), c),
            )
            copy.start()
            zout_copies.append(copy)
    zown[...] = of_x(term_x, klass)
    wait_z(2)
    wait_z(3)
    term_z[...] += product(tz, uz, ZFIRST[2])
    xout_copies = []
    for i, s in enumerate((2, 1, 3)):
        xout[i] = of_x(term_z, at_x(s)).astype(BF16)
        copy = remote(
            xout.at[i], xin.at[i], x_send.at[i], x_rcv.at[i], dev(at_x(s), y, z, c)
        )
        copy.start()
        xout_copies.append(copy)
    xown[...] = of_x(term_z, x)

    arrived(1)
    pass_on(1)
    arrived(2)
    pass_on(2)
    multiply(1, c)
    multiply(2, c)
    arrived_core(0)
    multiply(0, oc)
    arrived_core(3)
    multiply(3, oc)

    upper = lax.broadcasted_iota(jnp.int32, (8, KV), 0) < 4

    def regroup(total, first_ylo):
        for j in range(2):
            low, high = [], []
            for k in range(2):
                row = j * 32 + k * 16
                a, b = total[row : row + 8, :], total[row + 8 : row + 16, :]
                low.append(jnp.where(upper, a, pltpu.roll(b, 4, 0)))
                high.append(jnp.where(upper, pltpu.roll(a, 4, 0), b))
            ysend[first_ylo + j] = jnp.concatenate(low, axis=0).astype(BF16)
            ysend[LO + first_ylo + j] = jnp.concatenate(high, axis=0).astype(BF16)

    for copy in zout_copies:
        copy.wait_recv()
    regroup(
        (zown[...] + zin[0].astype(F32)) + (zin[1].astype(F32) + zin[2].astype(F32)), 0
    )
    for copy in xout_copies:
        copy.wait_recv()
    regroup(
        (xown[...] + xin[0].astype(F32)) + (xin[1].astype(F32) + xin[2].astype(F32)), 2
    )
    y_copies = []
    for s in (4, 3, 5, 2, 6, 1, 7):
        copy = remote(
            ysend.at[at_y(s)], yrecv.at[s - 1], y_send.at[s - 1], y_rcv.at[s - 1],
            dev(x, at_y(s), z, c),
        )
        copy.start()
        y_copies.append(copy)

    arrived(4)
    pass_on(4)
    arrived(5)
    pass_on(5)
    multiply(4, c)
    multiply(5, c)
    arrived_core(1)
    multiply(1, oc)
    arrived_core(2)
    multiply(2, oc)

    for copy in y_copies:
        copy.wait_recv()
    total = ysend[y].astype(F32)
    for s in range(NY - 1):
        total += yrecv[s].astype(F32)
    fsend[0] = total[0:8, :]
    fsend[1] = total[8:16, :]
    f_copies = []
    for i in range(LO):
        copy = remote(
            fsend.at[i // 2], frecv.at[z // LO], f_send.at[i], f_rcv.at[z // LO], finals[i]
        )
        f_copies.append(copy)

        @pl.when(jnp.logical_not(final_self[i]))
        def _(copy=copy):
            copy.start()

        @pl.when(final_self[i])
        def _(i=i):
            frecv[z // LO] = fsend[i // 2]

    arrived_core(4)
    multiply(4, oc)
    arrived_core(5)
    multiply(5, oc)
    val_ref[...] = vacc[...].astype(BF16)
    out_copies = [
        pltpu.make_async_copy(tg_ref, tg_hbm, out_sem.at[0]),
        pltpu.make_async_copy(val_ref, val_hbm, out_sem.at[1]),
    ]
    for copy in out_copies:
        copy.start()

    for g in range(4):
        @pl.when(jnp.logical_not(source_self[g]))
        def _(g=g):
            remote(fsend.at[0], frecv.at[g], f_send.at[g], f_rcv.at[g], to_core).wait_recv()
    final = (frecv[0] + frecv[1]) + (frecv[2] + frecv[3])
    wg_ref[...] = jnp.where(lax.rem(z, 2) == 0, final[0:4, :], final[4:8, :])

    for copy in (
        core_copies + tx_copies + tz_copies + ux_copies + uz_copies + [up_own] + uc_copies
        + w_copies + zout_copies + xout_copies + y_copies
    ):
        copy.wait_send()
    for i in range(LO):
        @pl.when(jnp.logical_not(final_self[i]))
        def _(i=i):
            f_copies[i].wait_send()
    for copy in out_copies:
        copy.wait()


def writer(val_in, tg_in, wg_in, val_out, tg_out, wg_out, val, tg, wg, in_sem, out_sem):
    pieces = [(val_in, val, val_out), (wg_in, wg, wg_out)]
    for i in range(4):
        rows = pl.ds(i * (TOK // 4), TOK // 4)
        pieces.append((tg_in.at[rows], tg.at[rows], tg_out.at[rows]))
    ins = [pltpu.make_async_copy(a, b, in_sem.at[i]) for i, (a, b, _) in enumerate(pieces)]
    outs = [pltpu.make_async_copy(b, c, out_sem.at[i]) for i, (_, b, c) in enumerate(pieces)]
    for copy in ins:
        copy.start()
    for i, copy in enumerate(ins):
        copy.wait()
        outs[i].start()
    for copy in outs:
        copy.wait()


def write_out(results):
    any_space = pl.BlockSpec(memory_space=pltpu.HBM)
    return pl.pallas_call(
        writer,
        out_shape=tuple(jax.ShapeDtypeStruct(r.shape, r.dtype) for r in results),
        in_specs=[any_space] * 3,
        out_specs=(any_space,) * 3,
        scratch_shapes=[pltpu.VMEM(r.shape, r.dtype) for r in results]
        + [pltpu.SemaphoreType.DMA((6,))] * 2,
        compiler_params=pltpu.CompilerParams(vmem_limit_bytes=60 * 1024 * 1024),
    )(*results)


def body(tokens, weight_codes, weight_scales, grad_codes, grad_scales):
    any_space = pl.BlockSpec(memory_space=pltpu.HBM)
    vmem = pl.BlockSpec(memory_space=pltpu.VMEM)
    dma = pltpu.SemaphoreType.DMA
    results = pl.pallas_call(
        kernel,
        out_shape=(
            jax.ShapeDtypeStruct((TOK, KV), BF16),
            jax.ShapeDtypeStruct((TOK, D), BF16),
            jax.ShapeDtypeStruct((4, KV), F32),
        ),
        in_specs=[any_space, any_space, vmem, any_space, vmem],
        out_specs=(any_space, any_space, vmem),
        scratch_shapes=[
            pltpu.VMEM((TOK, KV), BF16),
            pltpu.VMEM((TOK, D), BF16),
            pltpu.VMEM((TOK, D), BF16),
            pltpu.VMEM((ROWS, KV), jnp.int32),
            pltpu.VMEM((TOK, KV), jnp.int32),
            pltpu.VMEM((8, ROWS, KV), BF16),
            pltpu.VMEM((1024, 256), BF16),
            pltpu.VMEM((1024, 256), BF16),
            pltpu.VMEM((1024, KV), BF16),
            pltpu.VMEM((1024, KV), BF16),
            pltpu.VMEM((TOK, KV), F32),
            pltpu.VMEM((256, KV), F32),
            pltpu.VMEM((256, KV), F32),
            pltpu.VMEM((3, 64, KV), BF16),
            pltpu.VMEM((3, 64, KV), BF16),
            pltpu.VMEM((64, KV), F32),
            pltpu.VMEM((3, 64, KV), BF16),
            pltpu.VMEM((3, 64, KV), BF16),
            pltpu.VMEM((64, KV), F32),
            pltpu.VMEM((NY, 16, KV), BF16),
            pltpu.VMEM((NY - 1, 16, KV), BF16),
            pltpu.VMEM((2, 8, KV), F32),
            pltpu.VMEM((4, 8, KV), F32),
        ]
        + [
            dma((n,))
            for n in (3, 4, 4, 4, 12, 12, 16, 16, 3, 3, 4, 4, 8, 8, 6, 6, 8, 8, 4, 4, 3, 3, 7, 7, 4, 4, 2)
        ],
        compiler_params=pltpu.CompilerParams(
            collective_id=0, has_side_effects=True, vmem_limit_bytes=60 * 1024 * 1024
        ),
    )(tokens, weight_codes, weight_scales, grad_codes, grad_scales.T)
    return write_out(results)


def solution(mesh):
    return jax.shard_map(
        body,
        mesh=mesh,
        in_specs=(
            P(("hst", "outer"), None),
            P("hst", None),
            P("hst", None),
            P(("hst", "outer"), None),
            P(("hst", "outer"), None),
        ),
        out_specs=(P(("hst", "outer"), None), P(("hst", "outer"), None), P(("hst", "outer"), None)),
        check_vma=False,
    )
```

time: 77.4 us -> 65 us (0.84)
  the two profiles are of different devices: /device:TPU:48 before, /device:TPU:8 now
where the time goes in v2:
time: 65 us; the launch traced here: 64.7 us
  Pallas kernels  64.1 us (99%)
    pallas_call x1, Pallas kernels, body(): pl.pallas_call(kernel, out_shape=(jax.ShapeDtypeStruct((TOK, KV), BF16),...  62 us
    pallas_call x1, Pallas kernels, write_out(): pl.pallas_call(writer, out_shape=tuple((jax.ShapeDtypeStruct(r.shape, r.d...  2.1 us

profile of v2, /device:TPU:8, one launch (start us, length us, event | category | flops | bytes accessed | tf_op | source)
XLA Modules:
  0.0 64.7 jit_solution(15461786338637646520)
XLA Ops:
  0.6 62.0 %shard_map.76 = (bf16[128,512]{1,0:T(8,128)(2,1)}, bf16[128,4096]{1,0:T(8,128)(2,1)}, f32[4,512]{1,0:T(4,128)}) custom-call(bf16[128,4096]{1,0:T(8,128)(2,1)} %tok_hbm.1, s32[512,512]{1,0:T(8,128)} %wc_hbm.1, f32[4,512]{1,0:T(4,128)} %ws_ref.1, s32[128,512]{1,0:T(8,128)} %gc_hbm.1, f32[4,128]{1,0:T(4,128)} %bitcast.1), custom_call_target="tpu_custom_call" | custom-call | tf_op jit(solution)/shard_map/pallas_call | solution.py:455
  62.6 2.1 %shard_map.77 = (bf16[128,512]{1,0:T(8,128)(2,1)}, bf16[128,4096]{1,0:T(8,128)(2,1)}, f32[4,512]{1,0:T(4,128)}) custom-call(bf16[128,512]{1,0:T(8,128)(2,1)} %get-tuple-element.6.val_in, bf16[128,4096]{1,0:T(8,128)(2,1)} %get-tuple-element.7.tg_in, f32[4,512]{1,0:T(4,128)} %get-tuple-element.8.wg_in), custom_call_target="tpu_custom_call" | custom-call | tf_op jit(solution)/shard_map/pallas_call | solution.py:440

commit v3 on v2

--- a/solution.py
+++ b/solution.py
@@ -16,9 +16,9 @@
 
 def kernel(
     tok_hbm, wc_hbm, ws_ref, gc_hbm, gs_ref,
-    val_hbm, tg_hbm, wg_ref,
+    val_hbm, tg_hbm, frecv,
     val_ref, tg_ref, tok, wc, gc, wbuf, tx, tz, ux, uz, vacc, term_x, term_z,
-    zout, zin, zown, xout, xin, xown, ysend, yrecv, fsend, frecv,
+    zout, zin, zown, xout, xin, xown, ysend, yrecv, fsend,
     in_sem, own_sem, core_tsend, core_trcv, tx_send, tx_rcv, tz_send, tz_rcv,
     ux_send, ux_rcv, uz_send, uz_rcv, uc_send, uc_rcv,
     wsend, wrcv, wcsend, wcrcv, z_send, z_rcv, x_send, x_rcv, y_send, y_rcv, f_send, f_rcv, out_sem,
@@ -85,16 +85,21 @@
         copy.start()
 
     barrier = pltpu.get_barrier_semaphore()
-    partners = [dev(x, y, z, oc)]
-    partners += [dev(x, at_y(s), z, c) for s in range(1, NY)]
+    partners = [dev(x, at_y(s), z, c) for s in (4, 3, 5, 2, 6, 1, 7)]
     partners += [dev(x, y, at_z(s), cc) for s in ZSTEPS for cc in (c, oc)]
-    partners += [dev(at_x(s), y, z, cc) for s in XSTEPS for cc in (c, oc)]
+    partners += [dev(at_x(s), y, z, cc) for s in (2, 1, 3) for cc in (c, oc)]
+    partners += [dev(x, y, z, oc)]
     for p in partners:
         signal(p)
     for p, same in zip(finals + sources, final_self + source_self):
         @pl.when(jnp.logical_not(same))
         def _(p=p):
             signal(p)
+    load_gc.wait()
+    scales = gs_ref[...].T
+    for k in range(HEADS):
+        lanes = slice(k * 128, (k + 1) * 128)
+        ux[0:TOK, lanes] = (gc[:, lanes].astype(F32) * scales[:, k : k + 1]).astype(BF16)
     pl.semaphore_wait(barrier, jnp.where(loner, len(partners) + 6, len(partners) + 8))
 
     core_copies, tx_copies, tz_copies = [], [], []
@@ -127,35 +132,35 @@
                     tz_send.at[4 * i + 2 * k + j], tz_rcv.at[4 * i + 2 * k + j],
                     dev(x, y, at_z(s), cc),
                 ))
-    for copy in tx_copies[8:] + tz_copies[8:] + core_copies:
-        copy.start()
-
-    load_gc.wait()
-    scales = gs_ref[...].T
-    for k in range(HEADS):
-        lanes = slice(k * 128, (k + 1) * 128)
-        ux[0:TOK, lanes] = (gc[:, lanes].astype(F32) * scales[:, k : k + 1]).astype(BF16)
+
     to_core = dev(x, y, z, oc)
     up_own = remote(
         ux.at[pl.ds(0, TOK)], ux.at[pl.ds(TOK, TOK)], uc_send.at[7], uc_rcv.at[7], to_core
     )
-    ux_copies = [
-        remote(
+    ux_copies, uz_copies = [], []
+    for i, s in enumerate((1, 3)):
+        ux_copies.append(remote(
             ux.at[pl.ds(0, TOK)], ux.at[pl.ds(XFIRST[i], TOK)],
             ux_send.at[i], ux_rcv.at[i], dev(at_x(s), y, z, c),
-        )
-        for i, s in enumerate(XSTEPS)
-    ]
-    uz_copies = [
-        remote(
-            ux.at[pl.ds(64 if s == -2 else 0, ZCOUNT[i])], uz.at[pl.ds(ZFIRST[i], ZCOUNT[i])],
+        ))
+    for i, s in enumerate((1, -1)):
+        uz_copies.append(remote(
+            ux.at[pl.ds(0, TOK)], uz.at[pl.ds(ZFIRST[i], TOK)],
             uz_send.at[i], uz_rcv.at[i], dev(x, y, at_z(s), c),
-        )
-        for i, s in enumerate(ZSTEPS)
-    ]
-    for copy in ux_copies + uz_copies + [up_own]:
-        copy.start()
-    for copy in tx_copies[:8] + tz_copies[:8]:
+        ))
+    for i, s in enumerate((1, 3)):
+        ux_copies.append(remote(
+            ux.at[pl.ds(XFIRST[i] + 64 * i, 64)], ux.at[pl.ds(XFIRST[2] + 64 * i, 64)],
+            ux_send.at[2 + i], ux_rcv.at[2 + i], dev(at_x(s), y, z, c),
+        ))
+    for i, s in enumerate((1, -1)):
+        uz_copies.append(remote(
+            uz.at[pl.ds(ZFIRST[i] + 64 * i, 64)], uz.at[pl.ds(ZFIRST[2 + i], 64)],
+            uz_send.at[2 + i], uz_rcv.at[2 + i], dev(x, y, at_z(s), c),
+        ))
+    for copy in ux_copies[:2] + uz_copies[:2] + [up_own]:
+        copy.start()
+    for copy in tx_copies[8:] + tz_copies[8:] + core_copies + tx_copies[:8] + tz_copies[:8]:
         copy.start()
     uc_copies = [
         remote(
@@ -170,6 +175,7 @@
         )
         for i in range(4)
     ]
+
 
     load_wc.wait()
     for b in range(ROWS // 128):
@@ -230,30 +236,34 @@
             (((0,), (0,)), ((), ())), preferred_element_type=F32,
         )
 
-    multiply(6, c)
-    multiply(7, c)
+    def up_pass_on(copy, i):
+        copy.wait_recv()
+        uc_copies[i].start()
+
+    for i in (0, 1):
+        ux_copies[i].wait_recv()
+        ux_copies[2 + i].start()
+        uc_copies[i].start()
+        uz_copies[i].wait_recv()
+        uz_copies[2 + i].start()
+        uc_copies[3 + i].start()
+
     arrived(0)
     send_w(left, 0, wsend.at[4], wrcv.at[4], to_right)
     pass_on(0)
     arrived(3)
     send_w(right, 1, wsend.at[5], wrcv.at[5], to_left)
     pass_on(3)
-
-    def up_pass_on(copy, i):
-        copy.wait_recv()
-        uc_copies[i].start()
-
-    for i in (0, 1):
-        up_pass_on(ux_copies[i], i)
-        up_pass_on(uz_copies[i], 3 + i)
-
+    multiply(6, c)
+    multiply(7, c)
     for copy in own_copies:
         copy.wait()
     for copy in core_copies + [up_own]:
         copy.wait_recv()
     term_x[...] = product(tx, ux, 0)
     term_z[...] = product(tz, ux, 0)
-    up_pass_on(ux_copies[2], 2)
+    ux_copies[2].wait_recv()
+    up_pass_on(ux_copies[3], 2)
     up_pass_on(uz_copies[2], 5)
     up_pass_on(uz_copies[3], 6)
     arrived_core(6)
@@ -370,12 +380,18 @@
     total = ysend[y].astype(F32)
     for s in range(NY - 1):
         total += yrecv[s].astype(F32)
-    fsend[0] = total[0:8, :]
-    fsend[1] = total[8:16, :]
+    narrow = lax.broadcasted_iota(jnp.int32, (8, 128), 0) < 4
+    for b in range(2):
+        t = [total[8 * b : 8 * b + 8, 128 * j : 128 * j + 128] for j in range(4)]
+        r = [pltpu.roll(a, 4, 0) for a in t]
+        low = [jnp.where(narrow, t[j], r[j + 1]) for j in (0, 2)]
+        high = [jnp.where(narrow, r[j], t[j + 1]) for j in (0, 2)]
+        fsend[2 * b] = jnp.concatenate(low, axis=0).astype(BF16)
+        fsend[2 * b + 1] = jnp.concatenate(high, axis=0).astype(BF16)
     f_copies = []
     for i in range(LO):
         copy = remote(
-            fsend.at[i // 2], frecv.at[z // LO], f_send.at[i], f_rcv.at[z // LO], finals[i]
+            fsend.at[i], frecv.at[z // LO], f_send.at[i], f_rcv.at[z // LO], finals[i]
         )
         f_copies.append(copy)
 
@@ -385,7 +401,9 @@
 
         @pl.when(final_self[i])
         def _(i=i):
-            frecv[z // LO] = fsend[i // 2]
+            copy = pltpu.make_async_copy(fsend.at[i], frecv.at[z // LO], f_rcv.at[z // LO])
+            copy.start()
+            copy.wait()
 
     arrived_core(4)
     multiply(4, oc)
@@ -403,8 +421,6 @@
         @pl.when(jnp.logical_not(source_self[g]))
         def _(g=g):
             remote(fsend.at[0], frecv.at[g], f_send.at[g], f_rcv.at[g], to_core).wait_recv()
-    final = (frecv[0] + frecv[1]) + (frecv[2] + frecv[3])
-    wg_ref[...] = jnp.where(lax.rem(z, 2) == 0, final[0:4, :], final[4:8, :])
 
     for copy in (
         core_copies + tx_copies + tz_copies + ux_copies + uz_copies + [up_own] + uc_copies
@@ -419,17 +435,29 @@
         copy.wait()
 
 
-def writer(val_in, tg_in, wg_in, val_out, tg_out, wg_out, val, tg, wg, in_sem, out_sem):
-    pieces = [(val_in, val, val_out), (wg_in, wg, wg_out)]
+def writer(val_in, tg_in, last_in, val_out, tg_out, wg_out, val, tg, last, wg, in_sem, out_sem):
+    pieces = [(last_in, last, wg_out), (val_in, val, val_out)]
     for i in range(4):
         rows = pl.ds(i * (TOK // 4), TOK // 4)
         pieces.append((tg_in.at[rows], tg.at[rows], tg_out.at[rows]))
     ins = [pltpu.make_async_copy(a, b, in_sem.at[i]) for i, (a, b, _) in enumerate(pieces)]
-    outs = [pltpu.make_async_copy(b, c, out_sem.at[i]) for i, (_, b, c) in enumerate(pieces)]
+    outs = [
+        pltpu.make_async_copy(wg if i == 0 else b, c, out_sem.at[i])
+        for i, (_, b, c) in enumerate(pieces)
+    ]
     for copy in ins:
         copy.start()
-    for i, copy in enumerate(ins):
-        copy.wait()
+    ins[0].wait()
+    final = (last[0].astype(F32) + last[1].astype(F32)) + (
+        last[2].astype(F32) + last[3].astype(F32)
+    )
+    for j in range(2):
+        block = final[8 * j : 8 * j + 8, :]
+        wg[:, 256 * j : 256 * j + 128] = block[0:4, :]
+        wg[:, 256 * j + 128 : 256 * j + 256] = pltpu.roll(block, 4, 0)[0:4, :]
+    outs[0].start()
+    for i in range(1, len(ins)):
+        ins[i].wait()
         outs[i].start()
     for copy in outs:
         copy.wait()
@@ -437,12 +465,18 @@
 
 def write_out(results):
     any_space = pl.BlockSpec(memory_space=pltpu.HBM)
+    shapes = (((TOK, KV), BF16), ((TOK, D), BF16), ((4, KV), F32))
     return pl.pallas_call(
         writer,
-        out_shape=tuple(jax.ShapeDtypeStruct(r.shape, r.dtype) for r in results),
+        out_shape=tuple(jax.ShapeDtypeStruct(*shape) for shape in shapes),
         in_specs=[any_space] * 3,
         out_specs=(any_space,) * 3,
-        scratch_shapes=[pltpu.VMEM(r.shape, r.dtype) for r in results]
+        scratch_shapes=[
+            pltpu.VMEM((TOK, KV), BF16),
+            pltpu.VMEM((TOK, D), BF16),
+            pltpu.VMEM((4, 16, 128), BF16),
+            pltpu.VMEM((4, KV), F32),
+        ]
         + [pltpu.SemaphoreType.DMA((6,))] * 2,
         compiler_params=pltpu.CompilerParams(vmem_limit_bytes=60 * 1024 * 1024),
     )(*results)
@@ -457,10 +491,10 @@
         out_shape=(
             jax.ShapeDtypeStruct((TOK, KV), BF16),
             jax.ShapeDtypeStruct((TOK, D), BF16),
-            jax.ShapeDtypeStruct((4, KV), F32),
+            jax.ShapeDtypeStruct((4, 16, 128), BF16),
         ),
         in_specs=[any_space, any_space, vmem, any_space, vmem],
-        out_specs=(any_space, any_space, vmem),
+        out_specs=(any_space, any_space, any_space),
         scratch_shapes=[
             pltpu.VMEM((TOK, KV), BF16),
             pltpu.VMEM((TOK, D), BF16),
@@ -483,12 +517,11 @@
             pltpu.VMEM((64, KV), F32),
             pltpu.VMEM((NY, 16, KV), BF16),
             pltpu.VMEM((NY - 1, 16, KV), BF16),
-            pltpu.VMEM((2, 8, KV), F32),
-            pltpu.VMEM((4, 8, KV), F32),
+            pltpu.VMEM((4, 16, 128), BF16),
         ]
         + [
             dma((n,))
-            for n in (3, 4, 4, 4, 12, 12, 16, 16, 3, 3, 4, 4, 8, 8, 6, 6, 8, 8, 4, 4, 3, 3, 7, 7, 4, 4, 2)
+            for n in (3, 4, 4, 4, 12, 12, 16, 16, 4, 4, 4, 4, 8, 8, 6, 6, 8, 8, 4, 4, 3, 3, 7, 7, 4, 4, 2)
         ],
         compiler_params=pltpu.CompilerParams(
             collective_id=0, has_side_effects=True, vmem_limit_bytes=60 * 1024 * 1024

time: 65 us -> 61.2 us (0.942)
  Pallas kernels: 64.1 us -> 60.3 us
    pallas_call x1, Pallas kernels: 62 us -> 58.2 us  [body(): pl.pallas_call(kernel, out_shape=(jax.ShapeDtypeStruct((TOK, KV), BF16),...]
where the time goes in v3:
time: 61.2 us; the launch traced here: 61 us
  Pallas kernels  60.3 us (99%)
  between operations  0.64 us (1%)
    pallas_call x1, Pallas kernels, body(): pl.pallas_call(kernel, out_shape=(jax.ShapeDtypeStruct((TOK, KV), BF16),...  58.2 us
    pallas_call x1, Pallas kernels, write_out(): pl.pallas_call(writer, out_shape=tuple((jax.ShapeDtypeStruct(*shape) for...  2.1 us

profile of v3, /device:TPU:8, one launch (start us, length us, event | category | flops | bytes accessed | tf_op | source)
XLA Modules:
  0.0 61.0 jit_solution(5411211261745787849)
XLA Ops:
  0.6 58.2 %shard_map.76 = (bf16[128,512]{1,0:T(8,128)(2,1)}, bf16[128,4096]{1,0:T(8,128)(2,1)}, bf16[4,16,128]{2,1,0:T(8,128)(2,1)}) custom-call(bf16[128,4096]{1,0:T(8,128)(2,1)} %tok_hbm.1, s32[512,512]{1,0:T(8,128)} %wc_hbm.1, f32[4,512]{1,0:T(4,128)} %ws_ref.1, s32[128,512]{1,0:T(8,128)} %gc_hbm.1, f32[4,128]{1,0:T(4,128)} %bitcast.1), custom_call_target="tpu_custom_call" | custom-call | tf_op jit(solution)/shard_map/pallas_call | solution.py:489
  58.9 2.1 %shard_map.77 = (bf16[128,512]{1,0:T(8,128)(2,1)}, bf16[128,4096]{1,0:T(8,128)(2,1)}, f32[4,512]{1,0:T(4,128)}) custom-call(bf16[128,512]{1,0:T(8,128)(2,1)} %get-tuple-element.6.val_in, bf16[128,4096]{1,0:T(8,128)(2,1)} %get-tuple-element.7.tg_in, bf16[4,16,128]{2,1,0:T(8,128)(2,1)} %get-tuple-element.8.last_in), custom_call_target="tpu_custom_call" | custom-call | tf_op jit(solution)/shard_map/pallas_call | solution.py:469

commit v4 on v3

--- a/solution.py
+++ b/solution.py
@@ -21,7 +21,7 @@
     zout, zin, zown, xout, xin, xown, ysend, yrecv, fsend,
     in_sem, own_sem, core_tsend, core_trcv, tx_send, tx_rcv, tz_send, tz_rcv,
     ux_send, ux_rcv, uz_send, uz_rcv, uc_send, uc_rcv,
-    wsend, wrcv, wcsend, wcrcv, z_send, z_rcv, x_send, x_rcv, y_send, y_rcv, f_send, f_rcv, out_sem,
+    wsend, wrcv, wcsend, wcrcv, z_send, z_rcv, x_send, x_rcv, y_send, y_rcv, f_send, f_rcv, out_sem, far1, far2, far3,
 ):
     h, o = lax.axis_index("hst"), lax.axis_index("outer")
     c, ylo = lax.rem(h, 2), h // 2
@@ -48,8 +48,8 @@
             device_id=to, device_id_type=pl.DeviceIdType.MESH,
         )
 
-    def signal(to):
-        pl.semaphore_signal(barrier, inc=1, device_id=to, device_id_type=pl.DeviceIdType.MESH)
+    def signal(sem, to):
+        pl.semaphore_signal(sem, inc=1, device_id=to, device_id_type=pl.DeviceIdType.MESH)
 
     by_x = ylo < 2
     final_x = jnp.where(by_x, klass, x)
@@ -60,7 +60,8 @@
     source_k = jnp.where(by_x, x, z // LO)
     sources = [dev(source_x, y, source_k + LO * g, c) for g in range(4)]
     source_self = [(source_x == x) & (source_k + LO * g == z) for g in range(4)]
-    loner = (final_x == x) & (final_q == z // LO)
+
+    to_left, to_right = dev(x, at_y(-1), z, c), dev(x, at_y(1), z, c)
 
     load_tok = pltpu.make_async_copy(tok_hbm, tok, in_sem.at[0])
     load_wc = pltpu.make_async_copy(wc_hbm, wc, in_sem.at[1])
@@ -85,22 +86,19 @@
         copy.start()
 
     barrier = pltpu.get_barrier_semaphore()
-    partners = [dev(x, at_y(s), z, c) for s in (4, 3, 5, 2, 6, 1, 7)]
-    partners += [dev(x, y, at_z(s), cc) for s in ZSTEPS for cc in (c, oc)]
-    partners += [dev(at_x(s), y, z, cc) for s in (2, 1, 3) for cc in (c, oc)]
-    partners += [dev(x, y, z, oc)]
+    partners = [dev(at_x(s), y, z, cc) for s in (2, 1, 3) for cc in (c, oc)]
+    partners += [dev(x, y, at_z(s), cc) for s in (2, -2, 1, -1) for cc in (c, oc)]
+    partners += [dev(x, at_y(1), z, c), dev(x, at_y(-1), z, c), dev(x, y, z, oc)]
     for p in partners:
-        signal(p)
-    for p, same in zip(finals + sources, final_self + source_self):
-        @pl.when(jnp.logical_not(same))
-        def _(p=p):
-            signal(p)
+        signal(barrier, p)
     load_gc.wait()
     scales = gs_ref[...].T
     for k in range(HEADS):
         lanes = slice(k * 128, (k + 1) * 128)
         ux[0:TOK, lanes] = (gc[:, lanes].astype(F32) * scales[:, k : k + 1]).astype(BF16)
-    pl.semaphore_wait(barrier, jnp.where(loner, len(partners) + 6, len(partners) + 8))
+    pl.semaphore_wait(barrier, len(partners))
+    for to in (dev(x, y, at_z(2), c), dev(x, y, at_z(-2), c), to_left, to_right):
+        signal(far1, to)
 
     core_copies, tx_copies, tz_copies = [], [], []
     for j in range(2):
@@ -186,7 +184,6 @@
         return wbuf.at[ylo_of * 2 + cc, pl.ds(half * HALF, HALF)]
 
     left, right, far = lax.rem(ylo + 3, LO), lax.rem(ylo + 1, LO), lax.rem(ylo + 2, LO)
-    to_left, to_right = dev(x, at_y(-1), z, c), dev(x, at_y(1), z, c)
     w_copies = []
 
     def send_w(which, half, ssem, rsem, to):
@@ -248,6 +245,11 @@
         uz_copies[2 + i].start()
         uc_copies[3 + i].start()
 
+    pl.semaphore_wait(far1, 4)
+    for to in (
+        dev(x, y, at_z(4), c), dev(x, y, at_z(-4), c), dev(x, at_y(2), z, c), dev(x, at_y(-2), z, c)
+    ):
+        signal(far2, to)
     arrived(0)
     send_w(left, 0, wsend.at[4], wrcv.at[4], to_right)
     pass_on(0)
@@ -321,6 +323,9 @@
         xout_copies.append(copy)
     xown[...] = of_x(term_z, x)
 
+    pl.semaphore_wait(far2, 4)
+    for s in range(1, NX):
+        signal(far3, dev(at_x(s), y, z, c))
     arrived(1)
     pass_on(1)
     arrived(2)
@@ -388,6 +393,7 @@
         high = [jnp.where(narrow, r[j], t[j + 1]) for j in (0, 2)]
         fsend[2 * b] = jnp.concatenate(low, axis=0).astype(BF16)
         fsend[2 * b + 1] = jnp.concatenate(high, axis=0).astype(BF16)
+    pl.semaphore_wait(far3, NX - 1)
     f_copies = []
     for i in range(LO):
         copy = remote(
@@ -522,7 +528,8 @@
         + [
             dma((n,))
             for n in (3, 4, 4, 4, 12, 12, 16, 16, 4, 4, 4, 4, 8, 8, 6, 6, 8, 8, 4, 4, 3, 3, 7, 7, 4, 4, 2)
-        ],
+        ]
+        + [pltpu.SemaphoreType.REGULAR] * 3,
         compiler_params=pltpu.CompilerParams(
             collective_id=0, has_side_effects=True, vmem_limit_bytes=60 * 1024 * 1024
         ),

time: 61.2 us -> 56.7 us (0.926)
  the two profiles are of different devices: /device:TPU:8 before, /device:TPU:2 now
where the time goes in v4:
time: 56.7 us; the launch traced here: 56.4 us
  Pallas kernels  55.7 us (98%)
  between operations  0.64 us (1%)
    pallas_call x1, Pallas kernels, body(): pl.pallas_call(kernel, out_shape=(jax.ShapeDtypeStruct((TOK, KV), BF16),...  53.6 us
    pallas_call x1, Pallas kernels, write_out(): pl.pallas_call(writer, out_shape=tuple((jax.ShapeDtypeStruct(*shape) for...  2.1 us

profile of v4, /device:TPU:2, one launch (start us, length us, event | category | flops | bytes accessed | tf_op | source)
XLA Modules:
  0.0 56.4 jit_solution(8952350541941017214)
XLA Ops:
  0.6 53.6 %shard_map.76 = (bf16[128,512]{1,0:T(8,128)(2,1)}, bf16[128,4096]{1,0:T(8,128)(2,1)}, bf16[4,16,128]{2,1,0:T(8,128)(2,1)}) custom-call(bf16[128,4096]{1,0:T(8,128)(2,1)} %tok_hbm.1, s32[512,512]{1,0:T(8,128)} %wc_hbm.1, f32[4,512]{1,0:T(4,128)} %ws_ref.1, s32[128,512]{1,0:T(8,128)} %gc_hbm.1, f32[4,128]{1,0:T(4,128)} %bitcast.1), custom_call_target="tpu_custom_call" | custom-call | tf_op jit(solution)/shard_map/pallas_call | solution.py:495
  54.3 2.1 %shard_map.77 = (bf16[128,512]{1,0:T(8,128)(2,1)}, bf16[128,4096]{1,0:T(8,128)(2,1)}, f32[4,512]{1,0:T(4,128)}) custom-call(bf16[128,512]{1,0:T(8,128)(2,1)} %get-tuple-element.6.val_in, bf16[128,4096]{1,0:T(8,128)(2,1)} %get-tuple-element.7.tg_in, bf16[4,16,128]{2,1,0:T(8,128)(2,1)} %get-tuple-element.8.last_in), custom_call_target="tpu_custom_call" | custom-call | tf_op jit(solution)/shard_map/pallas_call | solution.py:475

commit v5 on v4

--- a/solution.py
+++ b/solution.py
@@ -15,13 +15,13 @@
 
 
 def kernel(
-    tok_hbm, wc_hbm, ws_ref, gc_hbm, gs_ref,
+    tok_hbm, wc_hbm, ws_hbm, gc_hbm, gs_hbm,
     val_hbm, tg_hbm, frecv,
     val_ref, tg_ref, tok, wc, gc, wbuf, tx, tz, ux, uz, vacc, term_x, term_z,
-    zout, zin, zown, xout, xin, xown, ysend, yrecv, fsend,
+    zout, zin, zown, xout, xin, xown, ysend, yrecv, fsend, ws_ref, gs_ref,
     in_sem, own_sem, core_tsend, core_trcv, tx_send, tx_rcv, tz_send, tz_rcv,
     ux_send, ux_rcv, uz_send, uz_rcv, uc_send, uc_rcv,
-    wsend, wrcv, wcsend, wcrcv, z_send, z_rcv, x_send, x_rcv, y_send, y_rcv, f_send, f_rcv, out_sem, far1, far2, far3,
+    wsend, wrcv, wcsend, wcrcv, z_send, z_rcv, x_send, x_rcv, y_send, y_rcv, f_send, f_rcv, out_sem, far1, far2, far3, far4,
 ):
     h, o = lax.axis_index("hst"), lax.axis_index("outer")
     c, ylo = lax.rem(h, 2), h // 2
@@ -63,12 +63,20 @@
 
     to_left, to_right = dev(x, at_y(-1), z, c), dev(x, at_y(1), z, c)
 
+    barrier = pltpu.get_barrier_semaphore()
+    partners = [dev(at_x(s), y, z, cc) for s in (1, 3) for cc in (c, oc)]
+    partners += [dev(x, y, at_z(s), cc) for s in (1, -1) for cc in (c, oc)]
+    partners += [dev(x, at_y(1), z, c), dev(x, at_y(-1), z, c), dev(x, y, z, oc)]
+    for p in partners:
+        signal(barrier, p)
+
     load_tok = pltpu.make_async_copy(tok_hbm, tok, in_sem.at[0])
     load_wc = pltpu.make_async_copy(wc_hbm, wc, in_sem.at[1])
     load_gc = pltpu.make_async_copy(gc_hbm, gc, in_sem.at[2])
-    load_gc.start()
-    load_wc.start()
-    load_tok.start()
+    load_gs = pltpu.make_async_copy(gs_hbm, gs_ref, in_sem.at[3])
+    load_ws = pltpu.make_async_copy(ws_hbm, ws_ref, in_sem.at[4])
+    for copy in (load_gc, load_gs, load_wc, load_ws, load_tok):
+        copy.start()
 
     def columns(ylo_of, cc, q):
         return pl.ds(pl.multiple_of(((ylo_of * 2 + cc) * 4 + q) * 128, 128), 128)
@@ -85,19 +93,17 @@
     for copy in own_copies:
         copy.start()
 
-    barrier = pltpu.get_barrier_semaphore()
-    partners = [dev(at_x(s), y, z, cc) for s in (2, 1, 3) for cc in (c, oc)]
-    partners += [dev(x, y, at_z(s), cc) for s in (2, -2, 1, -1) for cc in (c, oc)]
-    partners += [dev(x, at_y(1), z, c), dev(x, at_y(-1), z, c), dev(x, y, z, oc)]
-    for p in partners:
-        signal(barrier, p)
     load_gc.wait()
+    load_gs.wait()
     scales = gs_ref[...].T
     for k in range(HEADS):
         lanes = slice(k * 128, (k + 1) * 128)
         ux[0:TOK, lanes] = (gc[:, lanes].astype(F32) * scales[:, k : k + 1]).astype(BF16)
     pl.semaphore_wait(barrier, len(partners))
-    for to in (dev(x, y, at_z(2), c), dev(x, y, at_z(-2), c), to_left, to_right):
+    for to in (
+        dev(x, y, at_z(1), c), dev(x, y, at_z(-1), c), dev(at_x(1), y, z, c), dev(at_x(3), y, z, c),
+        to_left, to_right,
+    ):
         signal(far1, to)
 
     core_copies, tx_copies, tz_copies = [], [], []
@@ -158,7 +164,14 @@
         ))
     for copy in ux_copies[:2] + uz_copies[:2] + [up_own]:
         copy.start()
-    for copy in tx_copies[8:] + tz_copies[8:] + core_copies + tx_copies[:8] + tz_copies[:8]:
+    for copy in tx_copies[:8] + tz_copies[:8] + core_copies:
+        copy.start()
+    pl.semaphore_wait(far1, 6)
+    for to in (
+        dev(x, y, at_z(2), c), dev(x, y, at_z(-2), c), dev(x, at_y(2), z, c), dev(x, at_y(-2), z, c)
+    ):
+        signal(far2, to)
+    for copy in tx_copies[8:] + tz_copies[8:]:
         copy.start()
     uc_copies = [
         remote(
@@ -176,6 +189,7 @@
 
 
     load_wc.wait()
+    load_ws.wait()
     for b in range(ROWS // 128):
         rows = slice(b * 128, (b + 1) * 128)
         wbuf[h, rows, :] = (wc[rows, :].astype(F32) * ws_ref[b : b + 1, :]).astype(BF16)
@@ -245,11 +259,9 @@
         uz_copies[2 + i].start()
         uc_copies[3 + i].start()
 
-    pl.semaphore_wait(far1, 4)
-    for to in (
-        dev(x, y, at_z(4), c), dev(x, y, at_z(-4), c), dev(x, at_y(2), z, c), dev(x, at_y(-2), z, c)
-    ):
-        signal(far2, to)
+    pl.semaphore_wait(far2, 4)
+    for s in (4, -4):
+        signal(far3, dev(x, y, at_z(s), c))
     arrived(0)
     send_w(left, 0, wsend.at[4], wrcv.at[4], to_right)
     pass_on(0)
@@ -309,7 +321,6 @@
             )
             copy.start()
             zout_copies.append(copy)
-    zown[...] = of_x(term_x, klass)
     wait_z(2)
     wait_z(3)
     term_z[...] += product(tz, uz, ZFIRST[2])
@@ -321,11 +332,12 @@
         )
         copy.start()
         xout_copies.append(copy)
+    zown[...] = of_x(term_x, klass)
     xown[...] = of_x(term_z, x)
 
-    pl.semaphore_wait(far2, 4)
+    pl.semaphore_wait(far3, 2)
     for s in range(1, NX):
-        signal(far3, dev(at_x(s), y, z, c))
+        signal(far4, dev(at_x(s), y, z, c))
     arrived(1)
     pass_on(1)
     arrived(2)
@@ -393,7 +405,7 @@
         high = [jnp.where(narrow, r[j], t[j + 1]) for j in (0, 2)]
         fsend[2 * b] = jnp.concatenate(low, axis=0).astype(BF16)
         fsend[2 * b + 1] = jnp.concatenate(high, axis=0).astype(BF16)
-    pl.semaphore_wait(far3, NX - 1)
+    pl.semaphore_wait(far4, NX - 1)
     f_copies = []
     for i in range(LO):
         copy = remote(
@@ -490,7 +502,6 @@
 
 def body(tokens, weight_codes, weight_scales, grad_codes, grad_scales):
     any_space = pl.BlockSpec(memory_space=pltpu.HBM)
-    vmem = pl.BlockSpec(memory_space=pltpu.VMEM)
     dma = pltpu.SemaphoreType.DMA
     results = pl.pallas_call(
         kernel,
@@ -499,7 +510,7 @@
             jax.ShapeDtypeStruct((TOK, D), BF16),
             jax.ShapeDtypeStruct((4, 16, 128), BF16),
         ),
-        in_specs=[any_space, any_space, vmem, any_space, vmem],
+        in_specs=[any_space] * 5,
         out_specs=(any_space, any_space, any_space),
         scratch_shapes=[
             pltpu.VMEM((TOK, KV), BF16),
@@ -524,12 +535,14 @@
             pltpu.VMEM((NY, 16, KV), BF16),
             pltpu.VMEM((NY - 1, 16, KV), BF16),
             pltpu.VMEM((4, 16, 128), BF16),
+            pltpu.VMEM((ROWS // 128, KV), F32),
+            pltpu.VMEM((HEADS, TOK), F32),
         ]
         + [
             dma((n,))
-            for n in (3, 4, 4, 4, 12, 12, 16, 16, 4, 4, 4, 4, 8, 8, 6, 6, 8, 8, 4, 4, 3, 3, 7, 7, 4, 4, 2)
+            for n in (5, 4, 4, 4, 12, 12, 16, 16, 4, 4, 4, 4, 8, 8, 6, 6, 8, 8, 4, 4, 3, 3, 7, 7, 4, 4, 2)
         ]
-        + [pltpu.SemaphoreType.REGULAR] * 3,
+        + [pltpu.SemaphoreType.REGULAR] * 4,
         compiler_params=pltpu.CompilerParams(
             collective_id=0, has_side_effects=True, vmem_limit_bytes=60 * 1024 * 1024
         ),

time: 56.7 us -> 55 us (0.970)
  the two profiles are of different devices: /device:TPU:2 before, /device:TPU:6 now
where the time goes in v5:
time: 55 us; the launch traced here: 54.8 us
  Pallas kernels  54.2 us (99%)
  between operations  0.64 us (1%)
    pallas_call x1, Pallas kernels, body(): pl.pallas_call(kernel, out_shape=(jax.ShapeDtypeStruct((TOK, KV), BF16),...  52.1 us
    pallas_call x1, Pallas kernels, write_out(): pl.pallas_call(writer, out_shape=tuple((jax.ShapeDtypeStruct(*shape) for...  2.1 us

profile of v5, /device:TPU:6, one launch (start us, length us, event | category | flops | bytes accessed | tf_op | source)
XLA Modules:
  0.0 54.8 jit_solution(16569353910646106048)
XLA Ops:
  0.6 52.1 %shard_map.76 = (bf16[128,512]{1,0:T(8,128)(2,1)}, bf16[128,4096]{1,0:T(8,128)(2,1)}, bf16[4,16,128]{2,1,0:T(8,128)(2,1)}) custom-call(bf16[128,4096]{1,0:T(8,128)(2,1)} %tok_hbm.1, s32[512,512]{1,0:T(8,128)} %wc_hbm.1, f32[4,512]{1,0:T(4,128)} %ws_hbm.1, s32[128,512]{1,0:T(8,128)} %gc_hbm.1, f32[4,128]{1,0:T(4,128)} %bitcast.1), custom_call_target="tpu_custom_call" | custom-call | tf_op jit(solution)/shard_map/pallas_call | solution.py:506
  52.7 2.1 %shard_map.77 = (bf16[128,512]{1,0:T(8,128)(2,1)}, bf16[128,4096]{1,0:T(8,128)(2,1)}, f32[4,512]{1,0:T(4,128)}) custom-call(bf16[128,512]{1,0:T(8,128)(2,1)} %get-tuple-element.6.val_in, bf16[128,4096]{1,0:T(8,128)(2,1)} %get-tuple-element.7.tg_in, bf16[4,16,128]{2,1,0:T(8,128)(2,1)} %get-tuple-element.8.last_in), custom_call_target="tpu_custom_call" | custom-call | tf_op jit(solution)/shard_map/pallas_call | solution.py:487

commit v6 on v5

--- a/solution.py
+++ b/solution.py
@@ -17,11 +17,11 @@
 def kernel(
     tok_hbm, wc_hbm, ws_hbm, gc_hbm, gs_hbm,
     val_hbm, tg_hbm, frecv,
-    val_ref, tg_ref, tok, wc, gc, wbuf, tx, tz, ux, uz, vacc, term_x, term_z,
+    val_ref, tg_ref, tok, tokp, wc, gc, wbuf, tx, tz, ux, uz, vacc, term_x, term_z,
     zout, zin, zown, xout, xin, xown, ysend, yrecv, fsend, ws_ref, gs_ref,
     in_sem, own_sem, core_tsend, core_trcv, tx_send, tx_rcv, tz_send, tz_rcv,
     ux_send, ux_rcv, uz_send, uz_rcv, uc_send, uc_rcv,
-    wsend, wrcv, wcsend, wcrcv, z_send, z_rcv, x_send, x_rcv, y_send, y_rcv, f_send, f_rcv, out_sem, far1, far2, far3, far4,
+    wsend, wrcv, wcsend, wcrcv, z_send, z_rcv, x_send, x_rcv, y_send, y_rcv, f_send, f_rcv, out_sem, far1, far2, far3,
 ):
     h, o = lax.axis_index("hst"), lax.axis_index("outer")
     c, ylo = lax.rem(h, 2), h // 2
@@ -51,16 +51,9 @@
     def signal(sem, to):
         pl.semaphore_signal(sem, inc=1, device_id=to, device_id_type=pl.DeviceIdType.MESH)
 
-    by_x = ylo < 2
-    final_x = jnp.where(by_x, klass, x)
-    final_q = jnp.where(by_x, x, klass)
-    finals = [dev(final_x, y, final_q * LO + i, c) for i in range(LO)]
-    final_self = [(final_x == x) & (final_q * LO + i == z) for i in range(LO)]
-    source_x = jnp.where(by_x, z // LO, x)
-    source_k = jnp.where(by_x, x, z // LO)
-    sources = [dev(source_x, y, source_k + LO * g, c) for g in range(4)]
-    source_self = [(source_x == x) & (source_k + LO * g == z) for g in range(4)]
-
+    finals = [dev(x, y, klass * LO + i, c) for i in range(LO)]
+    final_self = [klass * LO + i == z for i in range(LO)]
+    source_self = [z // LO + LO * g == z for g in range(4)]
     to_left, to_right = dev(x, at_y(-1), z, c), dev(x, at_y(1), z, c)
 
     barrier = pltpu.get_barrier_semaphore()
@@ -85,9 +78,6 @@
     for j in range(2):
         lanes = pl.ds(j * 128, 128)
         own_copies.append(pltpu.make_async_copy(
-            tok_hbm.at[:, columns(j, c, x)], tx.at[pl.ds(0, TOK), lanes], own_sem.at[j]
-        ))
-        own_copies.append(pltpu.make_async_copy(
             tok_hbm.at[:, columns(2 + j, c, klass)], tz.at[pl.ds(0, TOK), lanes], own_sem.at[2 + j]
         ))
     for copy in own_copies:
@@ -99,6 +89,21 @@
     for k in range(HEADS):
         lanes = slice(k * 128, (k + 1) * 128)
         ux[0:TOK, lanes] = (gc[:, lanes].astype(F32) * scales[:, k : k + 1]).astype(BF16)
+    load_tok.wait()
+    new = lax.broadcasted_iota(jnp.int32, (ROWS, ROWS), 1)
+    old = lax.broadcasted_iota(jnp.int32, (ROWS, ROWS), 0)
+    source = ((new & 127) >> 3) * 32 + (new >> 7) * 8 + (new & 7)
+    permute = jnp.where(old == source, 1.0, 0.0).astype(BF16)
+    for j in range(2):
+        for k in range(2):
+            first = (2 * j + k) * ROWS
+            mixed = jnp.dot(
+                tok[:, first : first + ROWS], permute, preferred_element_type=F32
+            ).astype(BF16)
+            for xx in range(NX):
+                tokp[k, :, xx * 256 + j * 128 : xx * 256 + (j + 1) * 128] = mixed[
+                    :, xx * 128 : (xx + 1) * 128
+                ]
     pl.semaphore_wait(barrier, len(partners))
     for to in (
         dev(x, y, at_z(1), c), dev(x, y, at_z(-1), c), dev(at_x(1), y, z, c), dev(at_x(3), y, z, c),
@@ -106,26 +111,30 @@
     ):
         signal(far1, to)
 
+    def of_owner(xx):
+        return pl.ds(pl.multiple_of(xx * 256, 256), 256)
+
     core_copies, tx_copies, tz_copies = [], [], []
     for j in range(2):
         lanes = pl.ds(j * 128, 128)
-        core_copies.append(remote(
-            tok_hbm.at[:, columns(j, oc, x)], tx.at[pl.ds(TOK, TOK), lanes],
-            core_tsend.at[j], core_trcv.at[j], dev(x, y, z, oc),
-        ))
         core_copies.append(remote(
             tok_hbm.at[:, columns(2 + j, oc, klass)], tz.at[pl.ds(TOK, TOK), lanes],
             core_tsend.at[2 + j], core_trcv.at[2 + j], dev(x, y, z, oc),
         ))
     for i, s in enumerate(XSTEPS):
         for k, cc in enumerate((c, oc)):
-            for j in range(2):
-                tx_copies.append(remote(
-                    tok_hbm.at[:, columns(j, cc, at_x(s))],
-                    tx.at[pl.ds(XFIRST[i] + k * XCOUNT[i], XCOUNT[i]), pl.ds(j * 128, 128)],
-                    tx_send.at[4 * i + 2 * k + j], tx_rcv.at[4 * i + 2 * k + j],
-                    dev(at_x(s), y, z, cc),
-                ))
+            tx_copies.append(remote(
+                tokp.at[cc, :, of_owner(at_x(s))],
+                tx.at[pl.ds(XFIRST[i] + k * XCOUNT[i], XCOUNT[i])],
+                tx_send.at[2 * i + k], tx_rcv.at[2 * i + k], dev(at_x(s), y, z, cc),
+            ))
+    own_x = pltpu.make_async_copy(
+        tokp.at[c, :, of_owner(x)], tx.at[pl.ds(0, TOK)], own_sem.at[0]
+    )
+    core_x = remote(
+        tokp.at[oc, :, of_owner(x)], tx.at[pl.ds(TOK, TOK)],
+        core_tsend.at[0], core_trcv.at[0], dev(x, y, z, oc),
+    )
     for i, s in enumerate(ZSTEPS):
         first = 64 if s == -2 else 0
         for k, cc in enumerate((c, oc)):
@@ -164,14 +173,18 @@
         ))
     for copy in ux_copies[:2] + uz_copies[:2] + [up_own]:
         copy.start()
-    for copy in tx_copies[:8] + tz_copies[:8] + core_copies:
-        copy.start()
+    for copy in tz_copies[:8] + core_copies:
+        copy.start()
+    for copy in tx_copies[:4] + [own_x, core_x]:
+        copy.start()
+    own_copies.append(own_x)
+    core_copies.append(core_x)
     pl.semaphore_wait(far1, 6)
     for to in (
         dev(x, y, at_z(2), c), dev(x, y, at_z(-2), c), dev(x, at_y(2), z, c), dev(x, at_y(-2), z, c)
     ):
         signal(far2, to)
-    for copy in tx_copies[8:] + tz_copies[8:]:
+    for copy in tx_copies[4:] + tz_copies[8:]:
         copy.start()
     uc_copies = [
         remote(
@@ -228,7 +241,6 @@
         which, half = where[i]
         send_w(which, half, wcsend.at[i], wcrcv.at[i], to_core)
 
-    load_tok.wait()
     vacc[...] = jnp.zeros_like(vacc)
 
     def multiply(i, cc):
@@ -288,7 +300,7 @@
     multiply(3, c)
 
     def wait_x(i):
-        for copy in tx_copies[4 * i : 4 * i + 4] + [uc_copies[i]]:
+        for copy in tx_copies[2 * i : 2 * i + 2] + [uc_copies[i]]:
             copy.wait_recv()
 
     def wait_z(i):
@@ -305,11 +317,15 @@
         rows = [term[pl.ds(pl.multiple_of(a * 32 + xx * 8, 8), 8), :] for a in range(8)]
         return jnp.concatenate(rows, axis=0)
 
+    def of_q(q):
+        rows = [term_x[pl.ds(pl.multiple_of(a * 128 + q * 32, 32), 32), :] for a in range(2)]
+        return jnp.concatenate(rows, axis=0)
+
     wait_x(2)
     term_x[...] += product(tx, ux, XFIRST[2])
     zout_copies = []
     for i, s in enumerate((2, 1, -1)):
-        zout[i] = of_x(term_x, lax.rem(at_z(s), LO)).astype(BF16)
+        zout[i] = of_q(lax.rem(at_z(s), LO)).astype(BF16)
         if s == 2:
             pieces = ((0, 32, 2, 2, 2), (32, 32, -2, 2, 3))
         else:
@@ -332,12 +348,10 @@
         )
         copy.start()
         xout_copies.append(copy)
-    zown[...] = of_x(term_x, klass)
+    zown[...] = of_q(klass)
     xown[...] = of_x(term_z, x)
 
     pl.semaphore_wait(far3, 2)
-    for s in range(1, NX):
-        signal(far4, dev(at_x(s), y, z, c))
     arrived(1)
     pass_on(1)
     arrived(2)
@@ -405,7 +419,6 @@
         high = [jnp.where(narrow, r[j], t[j + 1]) for j in (0, 2)]
         fsend[2 * b] = jnp.concatenate(low, axis=0).astype(BF16)
         fsend[2 * b + 1] = jnp.concatenate(high, axis=0).astype(BF16)
-    pl.semaphore_wait(far4, NX - 1)
     f_copies = []
     for i in range(LO):
         copy = remote(
@@ -516,6 +529,7 @@
             pltpu.VMEM((TOK, KV), BF16),
             pltpu.VMEM((TOK, D), BF16),
             pltpu.VMEM((TOK, D), BF16),
+            pltpu.VMEM((2, TOK, 1024), BF16),
             pltpu.VMEM((ROWS, KV), jnp.int32),
             pltpu.VMEM((TOK, KV), jnp.int32),
             pltpu.VMEM((8, ROWS, KV), BF16),
@@ -542,7 +556,7 @@
             dma((n,))
             for n in (5, 4, 4, 4, 12, 12, 16, 16, 4, 4, 4, 4, 8, 8, 6, 6, 8, 8, 4, 4, 3, 3, 7, 7, 4, 4, 2)
         ]
-        + [pltpu.SemaphoreType.REGULAR] * 4,
+        + [pltpu.SemaphoreType.REGULAR] * 3,
         compiler_params=pltpu.CompilerParams(
             collective_id=0, has_side_effects=True, vmem_limit_bytes=60 * 1024 * 1024
         ),

time: 55 us -> 54.7 us (level)
  the two profiles are of different devices: /device:TPU:6 before, /device:TPU:8 now
where the time goes in v6:
time: 54.7 us; the launch traced here: 54.5 us
  Pallas kernels  53.8 us (98%)
  between operations  0.64 us (1%)
    pallas_call x1, Pallas kernels, body(): pl.pallas_call(kernel, out_shape=(jax.ShapeDtypeStruct((TOK, KV), BF16),...  51.7 us
    pallas_call x1, Pallas kernels, write_out(): pl.pallas_call(writer, out_shape=tuple((jax.ShapeDtypeStruct(*shape) for...  2.1 us

profile of v6, /device:TPU:8, one launch (start us, length us, event | category | flops | bytes accessed | tf_op | source)
XLA Modules:
  0.0 54.5 jit_solution(1903051620066545900)
XLA Ops:
  0.6 51.7 %shard_map.76 = (bf16[128,512]{1,0:T(8,128)(2,1)}, bf16[128,4096]{1,0:T(8,128)(2,1)}, bf16[4,16,128]{2,1,0:T(8,128)(2,1)}) custom-call(bf16[128,4096]{1,0:T(8,128)(2,1)} %tok_hbm.1, s32[512,512]{1,0:T(8,128)} %wc_hbm.1, f32[4,512]{1,0:T(4,128)} %ws_hbm.1, s32[128,512]{1,0:T(8,128)} %gc_hbm.1, f32[4,128]{1,0:T(4,128)} %bitcast.1), custom_call_target="tpu_custom_call" | custom-call | tf_op jit(solution)/shard_map/pallas_call | solution.py:519
  52.4 2.1 %shard_map.77 = (bf16[128,512]{1,0:T(8,128)(2,1)}, bf16[128,4096]{1,0:T(8,128)(2,1)}, f32[4,512]{1,0:T(4,128)}) custom-call(bf16[128,512]{1,0:T(8,128)(2,1)} %get-tuple-element.6.val_in, bf16[128,4096]{1,0:T(8,128)(2,1)} %get-tuple-element.7.tg_in, bf16[4,16,128]{2,1,0:T(8,128)(2,1)} %get-tuple-element.8.last_in), custom_call_target="tpu_custom_call" | custom-call | tf_op jit(solution)/shard_map/pallas_call | solution.py:500
